TPU v7x, 256 devices: a whole 4x4x8 slice. The times are simulated.
256 devices in a mesh: gx: 16 (over x, z_lo, core), gy: 16 (over y, z_hi).
Axes of the slice: x: 4, y: 4, z: 8 (z_hi: 4, z_lo: 2; z = z_hi * 2 + z_lo), core: 2. Of those that a mesh axis runs over, the one named last changes fastest.
Arguments:
- positions: float32 [3, 32, 32, 4, 128], P(None, 'gx', 'gy'), may hold values from 0 to 64, as said below
- velocity: float32 [3, 32, 32, 4, 128], P(None, 'gx', 'gy'), may hold values from -4 to 4
- density: float32 [32, 32, 4, 128], P('gx', 'gy'), may hold values from 0.8 to 1.2
- mass: float32 [32, 32, 4, 128], P('gx', 'gy'), may hold values from 0.05 to 0.15
- kind: int32 [32, 32, 4, 128], P('gx', 'gy'), may hold values from 0 to 2, as said below
Outputs:
- density_rate: float32 [32, 32, 4, 128], P('gx', 'gy')
- acceleration: float32 [3, 32, 32, 4, 128], P(None, 'gx', 'gy')
Inputs may be any that keep to these rules, and one draw needn't show every extreme that they name: `kind`: in every cell the particles fill the first slots and the rest are empty (0); each cell holds at least 32 particles; particles in the lowest layer of cells (third index 0) are boundary particles (2), all others fluid (1). positions[:, i, j, k, s] lies in the cube of side 2 whose lowest corner is 2 * (i, j, k).
All inputs are finite; a program needn't handle non-finite values.
Results may differ from a plain program's by a relative error of at most 0.000036.
Values sent between devices are 32-bit elements; how exact they have to be, the bound alone decides.
A program may use at most 192 MiB of HBM per device.

v0:
```python
import functools
import math

import jax
import jax.numpy as jnp
from jax import lax
from jax.experimental import pallas as pl
from jax.experimental.pallas import tpu as pltpu
from jax.sharding import PartitionSpec as P

MESH = pl.DeviceIdType.MESH
KERNEL_NORM = 21.0 / (16.0 * math.pi)
SCALE = -5.0 * KERNEL_NORM
STIFF = 9.0 / 7.0
DELTA_SOUND = 0.3
ALPHA_SOUND = 0.3
FLOOR = 0.25
GRAVITY = 1.0
SOFT4 = 0.0025

F32 = jnp.float32
BF16 = jnp.bfloat16
RAW = 80
SIDES = [(i, j) for i in (-1, 0, 1) for j in (-1, 0, 1) if (i, j) != (0, 0)]
TINY = 1e-12
HALVES = {0: ((0, 256), (0, 256), (128, 128)), 1: ((0, 128), (0, 256), (0, 256))}


def pieces(x):
    a = x.astype(BF16).astype(F32)
    r = x - a
    b = r.astype(BF16).astype(F32)
    return a, b, r - b


def power7(r):
    r2 = r * r
    r4 = r2 * r2
    return STIFF * (r4 * r2 * r - 1.0)


def distance_rows(xs, source):
    half = [0.5 * x for x in xs]
    cut = [pieces(h) for h in half]
    norm = pieces(half[0] * half[0] + half[1] * half[1] + half[2] * half[2])
    one = jnp.ones_like(half[0])
    rows = []
    for i in range(3):
        for j in range(3 - i):
            for d in range(3):
                rows.append(-2.0 * cut[d][i] if source else cut[d][j])
    rows += list(norm) + [one] * 3 if source else [one] * 3 + list(norm)
    return rows


def kernel(comm, pos_ref, vel_ref, rho_ref, mass_ref, kind_ref, rate_ref, acc_ref,
           ext, gext, raw, traw, feat_c, feat_d, feat_g, far, near, chl, dhl, sums, parts, mask,
           send_sem, recv_sem, gsend_sem, grecv_sem):
    if comm:
        gx = lax.axis_index("gx")
        gy = lax.axis_index("gy")
        nx = lax.axis_size("gx")
        ny = lax.axis_size("gy")
    else:
        gx, gy, nx, ny = jnp.int32(1), jnp.int32(1), 16, 16

    def peer(i, j):
        return (lax.rem(gx + i + nx, nx), lax.rem(gy + j + ny, ny))

    if comm:
        barrier = pltpu.get_barrier_semaphore()
        for i, j in SIDES:
            pl.semaphore_signal(barrier, inc=1, device_id=peer(i, j), device_id_type=MESH)

    kind = kind_ref[...]
    rho = rho_ref[...]
    vol = jnp.where(kind > 0, mass_ref[...], 0.0) / rho * SCALE
    own = [pos_ref[0], pos_ref[1], pos_ref[2], vel_ref[0], vel_ref[1], vel_ref[2], rho - 1.0, vol]

    def place(buf, rows, values):
        for a in range(2):
            for b in range(2):
                base = ((a + 1) * 4 + b + 1) * rows
                for ch, value in enumerate(values):
                    at = (a * 2 + b) * 4
                    buf[base + ch * 4:base + ch * 4 + 4, :] = value[at:at + 4, :]

    place(ext, 32, own)

    def swap(buf, rows, ssem, rsem):
        copies = []
        n = 0
        for i, j in SIDES:
            avals = (0, 1) if i == 0 else ((1,) if i == 1 else (0,))
            bvals = (0, 1) if j == 0 else ((1,) if j == 1 else (0,))
            runs = []
            for a in avals:
                src = (a + 1) * 4 + bvals[0] + 1
                dst = (a + 1 - 2 * i) * 4 + bvals[0] + 1 - 2 * j
                runs.append((src, dst, len(bvals)))
            for src, dst, count in runs:
                copies.append(pltpu.make_async_remote_copy(
                    src_ref=buf.at[pl.ds(src * rows, count * rows)],
                    dst_ref=buf.at[pl.ds(dst * rows, count * rows)],
                    send_sem=ssem.at[n], recv_sem=rsem.at[n],
                    device_id=peer(i, j), device_id_type=MESH))
                n += 1
        return copies

    if comm:
        pl.semaphore_wait(barrier, 8)
        moves = swap(ext, 32, send_sem, recv_sem)
        for c in moves:
            c.start()

    row = lax.broadcasted_iota(jnp.int32, (16, 128), 0)
    upper = lax.rem(row, 4) >= 2
    ox = ((gx * 2 + 1) * 2).astype(F32)
    oy = ((gy * 2 + 1) * 2).astype(F32)
    xt = [own[0] - ox, own[1] - oy, own[2] - jnp.where(upper, 6.0, 2.0)]
    for k, value in enumerate(distance_rows(xt, False)):
        for h in range(2):
            traw[pl.ds(h * 8 * 24 + k, 8, stride=24), :] = value[h * 8:h * 8 + 8]
    zeros = jnp.zeros((128, 256), BF16)
    for t in range(8):
        near[t] = zeros
        both = jnp.concatenate([traw[(2 * t + h) * 24:(2 * t + h + 1) * 24, :] for h in range(2)], axis=1)
        near[t, 0:32, :] = jnp.concatenate([both, jnp.zeros((8, 256), F32)], axis=0).astype(BF16)

    if comm:
        for c in moves:
            c.wait()

    col = lax.broadcasted_iota(jnp.int32, (16, 128), 0)
    ca = col // 4
    cb = lax.rem(col, 4)
    inside = ((ca > 0) | (gx > 0)) & ((ca < 3) | (gx < nx - 1)) & ((cb > 0) | (gy > 0)) & ((cb < 3) | (gy < ny - 1))

    def chan(ch, layer):
        return ext[pl.ds(ch * 4 + layer, 16, stride=32), :]

    def put(buf, rows, p, l, f, value):
        for h in range(2):
            buf[pl.ds(((p * 16 + 8 * h) * 3 + l) * rows + f, 8, stride=3 * rows), :] = value[8 * h:8 * h + 8]

    for p in range(2):
        for l in range(3):
            layer = p + l
            x = [chan(0, layer) - ox, chan(1, layer) - oy, chan(2, layer) - (6.0 if p else 2.0)]
            v = [chan(3 + d, layer) for d in range(3)]
            r = chan(6, layer)
            w = jnp.where(inside, chan(7, layer), 0.0)
            pr = power7(r + 1.0)
            vx = v[0] * x[0] + v[1] * x[1] + v[2] * x[2]
            wx = [w * x[d] for d in range(3)]
            wxx = [wx[a] * x[b] for a in range(3) for b in range(a, 3)]
            wv = [w * v[d] for d in range(3)]
            wr = w * r
            wp = w * pr
            rows_c = [w] + wx + wxx + [wr] + [wr * x[d] for d in range(3)] + wv + [w * vx] + [wp] + [wp * x[d] for d in range(3)]
            zero = jnp.zeros_like(w)
            rows_c += [zero, zero]
            e = [pieces(w), pieces(wr)]
            rows_d = wv + wx + wxx + [wv[a] * x[b] for a in range(3) for b in range(3)] + [w * vx * x[d] for d in range(3)]
            rows_d += [e[0][0], e[1][0], e[0][1], e[1][1], e[0][2], e[1][2], zero, zero]
            rows = rows_c + rows_d + distance_rows(x, True)
            for f, value in enumerate(rows):
                put(raw, RAW, p, l, f, value)

    eye = (lax.broadcasted_iota(jnp.int32, (128, 128), 0) == lax.broadcasted_iota(jnp.int32, (128, 128), 1))
    eye16 = jnp.where(eye, 1.0, 0.0).astype(BF16)
    mask[0] = jnp.ones((128, 128), F32)
    mask[1] = jnp.where(eye, 0.0, 1.0)
    mask[2] = jnp.ones((128, 128), F32)

    @pl.loop(0, 96)
    def _(n):
        base = pl.multiple_of(n * RAW, 8)
        got = raw[pl.ds(base, RAW), :]
        c3 = pieces(got[0:24])
        feat_c[n] = jnp.concatenate(list(c3) + [jnp.zeros((8, 128), F32)], axis=0).astype(BF16)
        d3 = pieces(got[24:48])
        feat_d[n] = jnp.concatenate(list(d3) + [got[48:56]], axis=0).astype(BF16)
        dist = jnp.concatenate([got[56:80], jnp.zeros((104, 128), F32)], axis=0).astype(BF16)
        far[n] = lax.dot_general(eye16, dist, (((1,), (1,)), ((), ())), preferred_element_type=F32).astype(BF16)

    for t in range(8):
        sums[t] = jnp.zeros((160, 256), F32)
    for q in range(36):
        chl[q, 0, 512:768, 0:128] = jnp.zeros((256, 128), BF16)
        chl[q, 1, 0:256, 128:256] = jnp.zeros((256, 128), BF16)
    for db in range(3):
        dhl[0, db, 512:768, 0:128] = jnp.zeros((256, 128), BF16)
        dhl[1, db, 0:256, 128:256] = jnp.zeros((256, 128), BF16)

    def two(x):
        hi = x.astype(BF16)
        lo = (x - hi.astype(F32)).astype(BF16)
        return hi, lo

    @pl.loop(0, 12)
    def _(n):
        tc = n // 3
        da = lax.rem(n, 3)
        ta = tc // 2
        tb = lax.rem(tc, 2)
        for p in range(2):
            nt = near[tc * 2 + p]
            fc = []
            fd = []
            for db in range(3):
                col = (ta + da) * 4 + tb + db
                cell0 = (p * 16 + col) * 3
                q = n * 3 + db
                for l in range(3):
                    lane, width = HALVES[p][l]
                    d2 = jnp.dot(far[cell0 + l], nt[:, lane:lane + width], preferred_element_type=F32)
                    d2 = jnp.maximum(d2, TINY)
                    wedge = jnp.maximum(1.0 - d2 * lax.rsqrt(d2), 0.0)
                    c = wedge * wedge * wedge
                    d = c * pl.reciprocal(d2 + SOFT4, approx=True)
                    if db == 1 and l - p in (0, 1):
                        halves = [d[:, 0:128], d[:, 128:256]]
                        halves[l - p] = halves[l - p] * mask[da]
                        d = jnp.concatenate(halves, axis=1)
                    chi, clo = two(c)
                    chl[q, p, l * 256:l * 256 + 128, lane:lane + width] = chi
                    chl[q, p, l * 256 + 128:l * 256 + 256, lane:lane + width] = clo
                    dhi, dlo = two(d)
                    dhl[p, db, l * 256:l * 256 + 128, lane:lane + width] = dhi
                    dhl[p, db, l * 256 + 128:l * 256 + 256, lane:lane + width] = dlo
                    fc += [feat_c[cell0 + l]] * 2
                    fd += [feat_d[cell0 + l]] * 2
            lhs_c = jnp.concatenate(fc, axis=1)
            lhs_d = jnp.concatenate(fd, axis=1)
            rc = chl[pl.ds(n * 3, 3), p].reshape(2304, 256)
            rd = dhl[p].reshape(2304, 256)
            t = tc * 2 + p
            sums[t, 0:80, :] += jnp.dot(lhs_c, rc, preferred_element_type=F32)
            sums[t, 80:160, :] += jnp.dot(lhs_d, rd, preferred_element_type=F32)

    for t in range(8):
        for h in range(2):
            s = sums[t, :, h * 128:h * 128 + 128]
            base = (2 * t + h) * 56
            parts[base:base + 24, :] = s[0:24] + s[24:48] + s[48:72]
            parts[base + 24:base + 48, :] = s[80:104] + s[104:128] + s[128:152]
            parts[base + 48:base + 56, :] = s[152:160]

    def part(f, stride=56):
        return jnp.concatenate([parts[pl.ds(h * 8 * stride + f, 8, stride=stride), :] for h in range(2)], axis=0)

    def dot3(a, b):
        return a[0] * b[0] + a[1] * b[1] + a[2] * b[2]

    pc = [part(f) for f in range(22)]
    s0, s1, sr, srx, sv, svx, sp, spx = pc[0], pc[1:4], pc[10], pc[11:14], pc[14:17], pc[17], pc[18], pc[19:22]
    pair = {}
    n = 0
    for a in range(3):
        for b in range(a, 3):
            pair[a, b] = pair[b, a] = n
            n += 1
    mom = {}
    for a in range(3):
        for b in range(a, 3):
            m = -(pc[4 + pair[a, b]] - xt[a] * s1[b] - xt[b] * (s1[a] - xt[a] * s0))
            mom[a, b] = m + FLOOR if a == b else m
    rt = own[6]
    back = [s0 * xt[a] - s1[a] for a in range(3)]
    slope = [(sr * xt[a] - srx[a]) - rt * back[a] for a in range(3)]
    m00, m01, m02, m11, m12, m22 = mom[0, 0], mom[0, 1], mom[0, 2], mom[1, 1], mom[1, 2], mom[2, 2]
    c00 = m11 * m22 - m12 * m12
    c01 = m02 * m12 - m01 * m22
    c02 = m01 * m12 - m02 * m11
    c11 = m00 * m22 - m02 * m02
    c12 = m01 * m02 - m00 * m12
    c22 = m00 * m11 - m01 * m01
    det = m00 * c00 + m01 * c01 + m02 * c02
    grad = [(c00 * slope[0] + c01 * slope[1] + c02 * slope[2]) / det,
            (c01 * slope[0] + c11 * slope[1] + c12 * slope[2]) / det,
            (c02 * slope[0] + c12 * slope[1] + c22 * slope[2]) / det]

    place(gext, 16, grad)
    if comm:
        moves = swap(gext, 16, gsend_sem, grecv_sem)
        for c in moves:
            c.start()

    vt = own[3:6]
    pt = power7(rho)
    vtx = dot3(vt, xt)
    flow = dot3(sv, xt) - svx - vtx * s0 + dot3(vt, s1)
    pd = [part(24 + f) for f in range(30)]
    d0 = pd[24] + pd[26] + pd[28]
    dr = pd[25] + pd[27] + pd[29]
    dv, d1, dxx, dvx, dvxx = pd[0:3], pd[3:6], pd[6:12], [pd[12:15], pd[15:18], pd[18:21]], pd[21:24]
    spread = -2.0 * ((sr - rt * s0) - SOFT4 * (dr - rt * d0))
    trace = dvx[0][0] + dvx[1][1] + dvx[2][2]
    head = dot3(dv, xt) - trace - vtx * d0 + dot3(vt, d1)
    push = []
    for b in range(3):
        tail = (xt[0] * dvx[0][b] + xt[1] * dvx[1][b] + xt[2] * dvx[2][b] - dvxx[b] - vtx * d1[b]
                + vt[0] * dxx[pair[0, b]] + vt[1] * dxx[pair[1, b]] + vt[2] * dxx[pair[2, b]])
        push.append(-(pt * back[b] + (sp * xt[b] - spx[b])) - (0.25 * ALPHA_SOUND) * (xt[b] * head - tail))
    moving = kind == 1
    for b in range(3):
        force = push[b] / rho - (GRAVITY if b == 2 else 0.0)
        acc_ref[b] = jnp.where(moving, force, 0.0)
    spread = spread - dot3(grad, back)

    if comm:
        for c in moves:
            c.wait()

    for p in range(2):
        for l in range(3):
            layer = p + l
            x = [chan(0, layer) - ox, chan(1, layer) - oy, chan(2, layer) - (6.0 if p else 2.0)]
            w = jnp.where(inside, chan(7, layer), 0.0)
            g = [gext[pl.ds(d * 4 + layer, 16, stride=16), :] for d in range(3)]
            rows = [pieces(w * g[d]) for d in range(3)] + [pieces(w * dot3(g, x))]
            for k in range(3):
                for f in range(4):
                    put(raw, 16, p, l, k * 4 + f, rows[f][k])
            for f in range(12, 16):
                put(raw, 16, p, l, f, jnp.zeros_like(w))

    @pl.loop(0, 96)
    def _(n):
        feat_g[n] = raw[pl.ds(pl.multiple_of(n * 16, 16), 16), :].astype(BF16)

    for t in range(8):
        tc, p = t // 2, t % 2
        ta, tb = tc // 2, tc % 2
        fg = []
        for da in range(3):
            for db in range(3):
                for l in range(3):
                    fg += [feat_g[(p * 16 + (ta + da) * 4 + tb + db) * 3 + l]] * 2
        rc = chl[tc * 9:tc * 9 + 9, p].reshape(6912, 256)
        s = jnp.dot(jnp.concatenate(fg, axis=1), rc, preferred_element_type=F32)
        for h in range(2):
            parts[(2 * t + h) * 16:(2 * t + h + 1) * 16, :] = s[:, h * 128:h * 128 + 128]
    q = [part(f, 16) for f in range(12)]
    q = [q[f] + q[f + 4] + q[f + 8] for f in range(4)]
    spread = spread - (dot3(q, xt) - q[3])
    rate = -rho * flow + DELTA_SOUND * spread
    rate_ref[...] = jnp.where(kind > 0, rate, 0.0)


def local(comm, positions, velocity, density, mass, kind):
    vmem = pl.BlockSpec(memory_space=pltpu.VMEM)
    dma = pltpu.SemaphoreType.DMA
    rate, acc = pl.pallas_call(
        functools.partial(kernel, comm),
        out_shape=(jax.ShapeDtypeStruct((16, 128), F32), jax.ShapeDtypeStruct((3, 16, 128), F32)),
        in_specs=[vmem] * 5,
        out_specs=(vmem, vmem),
        scratch_shapes=[
            pltpu.VMEM((512, 128), F32),
            pltpu.VMEM((256, 128), F32),
            pltpu.VMEM((96 * RAW, 128), F32),
            pltpu.VMEM((16 * 24, 128), F32),
            pltpu.VMEM((96, 80, 128), BF16),
            pltpu.VMEM((96, 80, 128), BF16),
            pltpu.VMEM((96, 16, 128), BF16),
            pltpu.VMEM((96, 128, 128), BF16),
            pltpu.VMEM((8, 128, 256), BF16),
            pltpu.VMEM((36, 2, 768, 256), BF16),
            pltpu.VMEM((2, 3, 768, 256), BF16),
            pltpu.VMEM((8, 160, 256), F32),
            pltpu.VMEM((16 * 56, 128), F32),
            pltpu.VMEM((3, 128, 128), F32),
            dma((10,)), dma((10,)), dma((10,)), dma((10,)),
        ],
        compiler_params=pltpu.CompilerParams(
            vmem_limit_bytes=56 * 1024 * 1024,
            **(dict(collective_id=0, has_side_effects=True) if comm else {})),
        cost_estimate=pl.CostEstimate(flops=2 * 10**9, bytes_accessed=10**6, transcendentals=10**7),
    )(positions.reshape(3, 16, 128), velocity.reshape(3, 16, 128), density.reshape(16, 128),
      mass.reshape(16, 128), kind.reshape(16, 128))
    return rate.reshape(2, 2, 4, 128), acc.reshape(3, 2, 2, 4, 128)


def solution(mesh):
    in_specs = (
        P(None, "gx", "gy", None, None),
        P(None, "gx", "gy", None, None),
        P("gx", "gy", None, None),
        P("gx", "gy", None, None),
        P("gx", "gy", None, None),
    )
    out_specs = (P("gx", "gy", None, None), P(None, "gx", "gy", None, None))
    return jax.shard_map(functools.partial(local, True), mesh=mesh, in_specs=in_specs, out_specs=out_specs,
                         check_vma=False)
```

profile of v0, /device:TPU:1, one launch (start us, length us, event | category | flops | bytes accessed | tf_op | source)
XLA Modules:
  0.0 71.5 jit_solution(7124863237120683114)
XLA Ops:
  0.6 68.2 %shard_map.68 = (f32[16,128]{1,0:T(8,128)}, f32[3,16,128]{2,1,0:T(8,128)}) custom-call(f32[3,16,128]{2,1,0:T(8,128)} %bitcast.9, f32[3,16,128]{2,1,0:T(8,128)} %bitcast.10, f32[16,128]{1,0:T(8,128)} %bitcast.11, f32[16,128]{1,0:T(8,128)} %bitcast.12, s32[16,128]{1,0:T(8,128)} %bitcast.13), custom_call_target="tpu_custom_call" | custom-call | flops 2000000000 | bytes 1000000 | tf_op jit(solution)/shard_map/pallas_call | solution.py:355
  68.9 1.3 %copy.9 = f32[2,2,4,128]{3,2,1,0:T(4,128)} copy(f32[2,2,4,128]{3,2,1,0:T(4,128)} %bitcast.8) | data formatting | bytes 16384
  70.2 1.3 %copy.10 = f32[3,2,2,4,128]{4,3,2,1,0:T(4,128)} copy(f32[3,2,2,4,128]{4,3,2,1,0:T(4,128)} %bitcast.7) | data formatting | bytes 49152
where the time goes:
time: 71.8 us; the launch traced here: 71.5 us
  Pallas kernels  68.2 us (95%)
  local copies, waits for them, and re-layouts  2.64 us (4%)
    pallas_call x1, Pallas kernels, local(): pl.pallas_call(functools.partial(kernel, comm), out_shape=(jax.ShapeDtype...  68.2 us
    unnamed x2, local copies, waits for them, and re-layouts  2.64 us

commit v1 on v0

v1 whole, which is shorter than its diff:
```python
import functools
import math

import jax
import jax.numpy as jnp
from jax import lax
from jax.experimental import pallas as pl
from jax.experimental.pallas import tpu as pltpu
from jax.sharding import PartitionSpec as P

MESH = pl.DeviceIdType.MESH
KERNEL_NORM = 21.0 / (16.0 * math.pi)
SCALE = -5.0 * KERNEL_NORM
STIFF = 9.0 / 7.0
DELTA_SOUND = 0.3
ALPHA_SOUND = 0.3
FLOOR = 0.25
GRAVITY = 1.0
SOFT4 = 0.0025

F32 = jnp.float32
BF16 = jnp.bfloat16
RAW = 80
SIDES = [(i, j) for i in (-1, 0, 1) for j in (-1, 0, 1) if (i, j) != (0, 0)]
TINY = 1e-12
BOTH = {0: (0, 1), 1: (2, 3)}
ONE = {0: 2, 1: 1}
LANE = {0: 128, 1: 0}
CUT = 1


def pieces(x):
    a = x.astype(BF16).astype(F32)
    r = x - a
    b = r.astype(BF16).astype(F32)
    return a, b, r - b


def power7(r):
    r2 = r * r
    r4 = r2 * r2
    return STIFF * (r4 * r2 * r - 1.0)


def distance_rows(xs, source):
    half = [0.5 * x for x in xs]
    cut = [pieces(h) for h in half]
    norm = pieces(half[0] * half[0] + half[1] * half[1] + half[2] * half[2])
    one = jnp.ones_like(half[0])
    rows = []
    for i in range(3):
        for j in range(3 - i):
            for d in range(3):
                rows.append(-2.0 * cut[d][i] if source else cut[d][j])
    rows += list(norm) + [one] * 3 if source else [one] * 3 + list(norm)
    return rows


def kernel(comm, pos_ref, vel_ref, rho_ref, mass_ref, kind_ref, rate_ref, acc_ref,
           ext, gext, raw, traw, feat_c, feat_d, feat_g, far, near, cfull, chalf, dfull, dhalf, sums, parts, gsums, off,
           send_sem, recv_sem, gsend_sem, grecv_sem):
    if comm:
        gx = lax.axis_index("gx")
        gy = lax.axis_index("gy")
        nx = lax.axis_size("gx")
        ny = lax.axis_size("gy")
    else:
        gx, gy, nx, ny = jnp.int32(1), jnp.int32(1), 16, 16

    def peer(i, j):
        return (lax.rem(gx + i + nx, nx), lax.rem(gy + j + ny, ny))

    if comm:
        barrier = pltpu.get_barrier_semaphore()
        for i, j in SIDES:
            pl.semaphore_signal(barrier, inc=1, device_id=peer(i, j), device_id_type=MESH)

    kind = kind_ref[...]
    rho = rho_ref[...]
    vol = jnp.where(kind > 0, mass_ref[...], 0.0) / rho * SCALE
    own = [pos_ref[0], pos_ref[1], pos_ref[2], vel_ref[0], vel_ref[1], vel_ref[2], rho - 1.0, vol]

    def spread_rows(buf, start, stride, value):
        for h in range(value.shape[0] // 8):
            buf[pl.ds(start + h * 8 * stride, 8, stride=stride), :] = value[h * 8:h * 8 + 8]

    def take_rows(buf, start, stride, count):
        return jnp.concatenate([buf[pl.ds(start + h * 8 * stride, 8, stride=stride), :] for h in range(count // 8)], axis=0)

    for ch in range(8):
        spread_rows(ext, ch, 8, own[ch])

    def swap(buf, rows, ssem, rsem):
        moves = []
        for i, j in SIDES:
            if j == 0:
                a = 1 if i > 0 else 0
                runs = [(2 * a, 4 + 2 * (1 - a), 2)]
            elif i == 0:
                b = 1 if j > 0 else 0
                runs = [(2 * a + b, 8 + 2 * (1 - b) + a, 1) for a in range(2)]
            else:
                a, b = (1 if i > 0 else 0), (1 if j > 0 else 0)
                runs = [(2 * a + b, 12 + 2 * (1 - a) + 1 - b, 1)]
            for src, dst, count in runs:
                n = len(moves)
                moves.append(pltpu.make_async_remote_copy(
                    src_ref=buf.at[pl.ds(src * rows, count * rows)],
                    dst_ref=buf.at[pl.ds(dst * rows, count * rows)],
                    send_sem=ssem.at[n], recv_sem=rsem.at[n],
                    device_id=peer(i, j), device_id_type=MESH))
        return moves

    ox = ((gx * 2 + 1) * 2).astype(F32)
    oy = ((gy * 2 + 1) * 2).astype(F32)

    xt = [own[0] - ox, own[1] - oy, own[2] - 4.0]
    for k, value in enumerate(distance_rows(xt, False)):
        spread_rows(traw, k, 24, value)
    for t in range(8):
        p = t % 2
        both = jnp.concatenate([traw[(2 * t + h) * 24:(2 * t + h + 1) * 24, :] for h in range(2)], axis=1)
        both = jnp.concatenate([both, jnp.zeros((8, 256), F32)], axis=0).astype(BF16)
        blocks = [(BOTH[p][0], both), (BOTH[p][1], both), (ONE[p], both[:, LANE[p]:LANE[p] + 128])]
        near[t] = jnp.concatenate(
            [jnp.concatenate([b if ly == at else jnp.zeros_like(b) for ly in range(4)], axis=0) for at, b in blocks], axis=1)

    eye = (lax.broadcasted_iota(jnp.int32, (128, 128), 0) == lax.broadcasted_iota(jnp.int32, (128, 128), 1))
    eye16 = jnp.where(eye, 1.0, 0.0).astype(BF16)
    off[...] = jnp.where(eye, 0.0, 1.0)

    def features(first, count, inside):
        def chan(ch):
            return take_rows(ext, first * 8 + ch, 8, count)

        x = [chan(0) - ox, chan(1) - oy, chan(2) - 4.0]
        v = [chan(3 + d) for d in range(3)]
        r = chan(6)
        w = chan(7)
        if inside is not None:
            w = jnp.where(inside, w, 0.0)
        pr = power7(r + 1.0)
        vx = v[0] * x[0] + v[1] * x[1] + v[2] * x[2]
        wx = [w * x[d] for d in range(3)]
        wxx = [wx[a] * x[b] for a in range(3) for b in range(a, 3)]
        wv = [w * v[d] for d in range(3)]
        wr = w * r
        wp = w * pr
        zero = jnp.zeros_like(w)
        rows = [w] + wx + wxx + [wr] + [wr * x[d] for d in range(3)] + wv + [w * vx] + [wp] + [wp * x[d] for d in range(3)]
        rows += [zero, zero]
        e, f = pieces(w), pieces(wr)
        rows += wv + wx + wxx + [wv[a] * x[b] for a in range(3) for b in range(3)] + [w * vx * x[d] for d in range(3)]
        rows += [e[0], f[0], e[1], f[1], e[2], f[2], zero, zero]
        rows += distance_rows(x, True)
        for f, value in enumerate(rows):
            spread_rows(raw, first * RAW + f, RAW, value)

    def column(c):
        dist = []
        for layer in range(4):
            cell = c * 4 + layer
            got = raw[pl.ds(pl.multiple_of(cell * RAW, 8), RAW), :]
            feat_c[cell] = jnp.concatenate(list(pieces(got[0:24])) + [jnp.zeros((8, 128), F32)], axis=0).astype(BF16)
            feat_d[cell] = jnp.concatenate(list(pieces(got[24:48])) + [got[48:56]], axis=0).astype(BF16)
            dist += [got[56:80], jnp.zeros((8, 128), F32)]
        dist = jnp.concatenate(dist, axis=0).astype(BF16)
        far[c] = lax.dot_general(eye16, dist, (((1,), (1,)), ((), ())), preferred_element_type=F32).astype(BF16)

    def two(x):
        hi = x.astype(BF16)
        lo = (x - hi.astype(F32)).astype(BF16)
        return jnp.concatenate([hi, lo], axis=0)

    def weigh(tc, p, col, full_c, half_c, full_d, half_d, self_col):
        gap = jnp.dot(far[col], near[tc * 2 + p], preferred_element_type=F32)
        for k in range(3):
            d2 = jnp.maximum(gap[:, 256 * k:min(256 * k + 256, 640)], TINY)
            wedge = jnp.maximum(1.0 - d2 * lax.rsqrt(d2), 0.0)
            c = wedge * wedge * wedge
            d = c * pl.reciprocal(d2 + SOFT4, approx=True)
            if self_col and k < 2:
                halves = [d[:, 0:128], d[:, 128:256]]
                halves[k] = halves[k] * off[...]
                d = jnp.concatenate(halves, axis=1)
            if k < 2:
                full_c[k * 256:k * 256 + 256] = two(c)
                full_d[k * 256:k * 256 + 256] = two(d)
            else:
                half_c[...] = two(c)
                half_d[...] = two(d)

    def total(feat, rows, p, cols, full, half):
        lf, lh = [], []
        for c in cols:
            for ly in BOTH[p]:
                lf += [feat[c * 4 + ly]] * 2
            lh += [feat[c * 4 + ONE[p]]] * 2
        n = len(cols)
        f = jnp.dot(jnp.concatenate(lf, axis=1), full.reshape(n * 512, 256), preferred_element_type=F32)
        h = jnp.dot(jnp.concatenate(lh, axis=1), half.reshape(n * 256, 128), preferred_element_type=F32)
        return (f[:, 0:128], f[:, 128:256] + h) if p == 0 else (f[:, 0:128] + h, f[:, 128:256])

    def mates(tc):
        return [lax.rem(tc + k, 4) for k in range(4)]

    def halo(tc):
        a, b = tc // 2, lax.rem(tc, 2)
        return [4 + 2 * a, 5 + 2 * a, 8 + 2 * b, 9 + 2 * b, 12 + tc]

    def fold(s):
        return s[0:24] + s[24:48] + s[48:72]

    features(0, 16, None)
    for c in range(4):
        column(c)

    def own_pairs(tc):
        for p in range(2):
            cols = mates(tc)
            for k in range(4):
                weigh(tc, p, cols[k], cfull.at[p, tc, k], chalf.at[p, tc, k], dfull.at[p, tc, k], dhalf.at[p, tc, k], k == 0)
            for which, (feat, full, half) in enumerate(((feat_c, cfull, chalf), (feat_d, dfull, dhalf))):
                got = total(feat, 80, p, cols, full[p, tc, 0:4], half[p, tc, 0:4])
                for h in range(2):
                    sums[tc * 2 + p, h, which * 80:which * 80 + 80] = got[h]

    pl.loop(0, CUT)(own_pairs)
    if comm:
        pl.semaphore_wait(barrier, 8)
        moves = swap(ext, 32, send_sem, recv_sem)
        for c in moves:
            c.start()
    pl.loop(CUT, 4)(own_pairs)
    if comm:
        for c in moves:
            c.wait()

    cell = lax.broadcasted_iota(jnp.int32, (48, 128), 0) // 4 + 4
    group = cell // 2
    below_a = (group == 2) | (cell == 12) | (cell == 13)
    above_a = (group == 3) | (cell == 14) | (cell == 15)
    below_b = (group == 4) | (cell == 12) | (cell == 14)
    above_b = (group == 5) | (cell == 13) | (cell == 15)
    outside = (below_a & (gx == 0)) | (above_a & (gx == nx - 1)) | (below_b & (gy == 0)) | (above_b & (gy == ny - 1))
    features(16, 48, jnp.logical_not(outside))

    @pl.loop(0, 3)
    def _(n):
        for k in range(4):
            column(4 + n * 4 + k)

    @pl.loop(0, 4)
    def _(tc):
        for p in range(2):
            cols = halo(tc)
            for k in range(5):
                weigh(tc, p, cols[k], cfull.at[p, tc, 4 + k], chalf.at[p, tc, 4 + k], dfull.at[p, tc, k],
                      dhalf.at[p, tc, k], False)
            got = total(feat_c, 80, p, cols, cfull[p, tc, 4:9], chalf[p, tc, 4:9])
            for h in range(2):
                base = pl.multiple_of((tc * 4 + p * 2 + h) * 56, 8)
                parts[pl.ds(base, 24), :] = fold(sums[tc * 2 + p, h, 0:80] + got[h])

    def part(f, stride=56):
        return take_rows(parts, f, stride, 16)

    def dot3(a, b):
        return a[0] * b[0] + a[1] * b[1] + a[2] * b[2]

    pc = [part(f) for f in range(22)]
    s0, s1, sr, srx, sv, svx, sp, spx = pc[0], pc[1:4], pc[10], pc[11:14], pc[14:17], pc[17], pc[18], pc[19:22]
    pair = {}
    n = 0
    for a in range(3):
        for b in range(a, 3):
            pair[a, b] = pair[b, a] = n
            n += 1
    mom = {}
    for a in range(3):
        for b in range(a, 3):
            m = -(pc[4 + pair[a, b]] - xt[a] * s1[b] - xt[b] * (s1[a] - xt[a] * s0))
            mom[a, b] = m + FLOOR if a == b else m
    rt = own[6]
    back = [s0 * xt[a] - s1[a] for a in range(3)]
    slope = [(sr * xt[a] - srx[a]) - rt * back[a] for a in range(3)]
    m00, m01, m02, m11, m12, m22 = mom[0, 0], mom[0, 1], mom[0, 2], mom[1, 1], mom[1, 2], mom[2, 2]
    c00 = m11 * m22 - m12 * m12
    c01 = m02 * m12 - m01 * m22
    c02 = m01 * m12 - m02 * m11
    c11 = m00 * m22 - m02 * m02
    c12 = m01 * m02 - m00 * m12
    c22 = m00 * m11 - m01 * m01
    det = m00 * c00 + m01 * c01 + m02 * c02
    grad = [(c00 * slope[0] + c01 * slope[1] + c02 * slope[2]) / det,
            (c01 * slope[0] + c11 * slope[1] + c12 * slope[2]) / det,
            (c02 * slope[0] + c12 * slope[1] + c22 * slope[2]) / det]

    for d in range(3):
        spread_rows(gext, d, 4, grad[d])
    if comm:
        moves = swap(gext, 16, gsend_sem, grecv_sem)
        for c in moves:
            c.start()

    @pl.loop(0, 4)
    def _(tc):
        for p in range(2):
            got = total(feat_d, 80, p, halo(tc), dfull[p, tc, 0:5], dhalf[p, tc, 0:5])
            for h in range(2):
                s = sums[tc * 2 + p, h, 80:160] + got[h]
                base = pl.multiple_of((tc * 4 + p * 2 + h) * 56, 8)
                parts[pl.ds(base + 24, 24), :] = fold(s)
                parts[pl.ds(base + 48, 8), :] = s[72:80]

    def slopes(first, count, inside):
        x = [take_rows(ext, first * 8 + d, 8, count) - o for d, o in enumerate((ox, oy, 4.0))]
        w = take_rows(ext, first * 8 + 7, 8, count)
        if inside is not None:
            w = jnp.where(inside, w, 0.0)
        g = [take_rows(gext, first * 4 + d, 4, count) for d in range(3)]
        rows = [pieces(w * g[d]) for d in range(3)] + [pieces(w * dot3(g, x))]
        for k in range(3):
            for f in range(4):
                spread_rows(raw, first * 16 + k * 4 + f, 16, rows[f][k])
        for f in range(12, 16):
            spread_rows(raw, first * 16 + f, 16, jnp.zeros_like(w))
        for n in range(first, first + count):
            feat_g[n] = raw[n * 16:n * 16 + 16, :].astype(BF16)

    slopes(0, 16, None)

    @pl.loop(0, 4)
    def _(tc):
        for p in range(2):
            got = total(feat_g, 16, p, mates(tc), cfull[p, tc, 0:4], chalf[p, tc, 0:4])
            for h in range(2):
                gsums[tc * 2 + p, h] = got[h]

    vt = own[3:6]
    pt = power7(rho)
    vtx = dot3(vt, xt)
    flow = dot3(sv, xt) - svx - vtx * s0 + dot3(vt, s1)
    pd = [part(24 + f) for f in range(30)]
    d0 = pd[24] + pd[26] + pd[28]
    dr = pd[25] + pd[27] + pd[29]
    dv, d1, dxx, dvx, dvxx = pd[0:3], pd[3:6], pd[6:12], [pd[12:15], pd[15:18], pd[18:21]], pd[21:24]
    spread = -2.0 * ((sr - rt * s0) - SOFT4 * (dr - rt * d0))
    trace = dvx[0][0] + dvx[1][1] + dvx[2][2]
    head = dot3(dv, xt) - trace - vtx * d0 + dot3(vt, d1)
    push = []
    for b in range(3):
        tail = (xt[0] * dvx[0][b] + xt[1] * dvx[1][b] + xt[2] * dvx[2][b] - dvxx[b] - vtx * d1[b]
                + vt[0] * dxx[pair[0, b]] + vt[1] * dxx[pair[1, b]] + vt[2] * dxx[pair[2, b]])
        push.append(-(pt * back[b] + (sp * xt[b] - spx[b])) - (0.25 * ALPHA_SOUND) * (xt[b] * head - tail))
    moving = kind == 1
    for b in range(3):
        force = push[b] / rho - (GRAVITY if b == 2 else 0.0)
        acc_ref[b] = jnp.where(moving, force, 0.0)
    spread = spread - dot3(grad, back)

    if comm:
        for c in moves:
            c.wait()
    slopes(16, 48, jnp.logical_not(outside))

    @pl.loop(0, 4)
    def _(tc):
        for p in range(2):
            got = total(feat_g, 16, p, halo(tc), cfull[p, tc, 4:9], chalf[p, tc, 4:9])
            for h in range(2):
                base = pl.multiple_of((tc * 4 + p * 2 + h) * 16, 8)
                parts[pl.ds(base, 16), :] = gsums[tc * 2 + p, h] + got[h]

    q = [part(f, 16) for f in range(12)]
    q = [q[f] + q[f + 4] + q[f + 8] for f in range(4)]
    spread = spread - (dot3(q, xt) - q[3])
    rate = -rho * flow + DELTA_SOUND * spread
    rate_ref[...] = jnp.where(kind > 0, rate, 0.0)


def local(comm, positions, velocity, density, mass, kind):
    vmem = pl.BlockSpec(memory_space=pltpu.VMEM)
    dma = pltpu.SemaphoreType.DMA
    rate, acc = pl.pallas_call(
        functools.partial(kernel, comm),
        out_shape=(jax.ShapeDtypeStruct((16, 128), F32), jax.ShapeDtypeStruct((3, 16, 128), F32)),
        in_specs=[vmem] * 5,
        out_specs=(vmem, vmem),
        scratch_shapes=[
            pltpu.VMEM((512, 128), F32),
            pltpu.VMEM((256, 128), F32),
            pltpu.VMEM((64 * RAW, 128), F32),
            pltpu.VMEM((16 * 24, 128), F32),
            pltpu.VMEM((64, 80, 128), BF16),
            pltpu.VMEM((64, 80, 128), BF16),
            pltpu.VMEM((64, 16, 128), BF16),
            pltpu.VMEM((16, 128, 128), BF16),
            pltpu.VMEM((8, 128, 640), BF16),
            pltpu.VMEM((2, 4, 9, 512, 256), BF16),
            pltpu.VMEM((2, 4, 9, 256, 128), BF16),
            pltpu.VMEM((2, 4, 5, 512, 256), BF16),
            pltpu.VMEM((2, 4, 5, 256, 128), BF16),
            pltpu.VMEM((8, 2, 160, 128), F32),
            pltpu.VMEM((16 * 56, 128), F32),
            pltpu.VMEM((8, 2, 16, 128), F32),
            pltpu.VMEM((128, 128), F32),
            dma((10,)), dma((10,)), dma((10,)), dma((10,)),
        ],
        compiler_params=pltpu.CompilerParams(
            vmem_limit_bytes=56 * 1024 * 1024,
            **(dict(collective_id=0, has_side_effects=True) if comm else {})),
        cost_estimate=pl.CostEstimate(flops=2 * 10**9, bytes_accessed=10**6, transcendentals=10**7),
    )(positions.reshape(3, 16, 128), velocity.reshape(3, 16, 128), density.reshape(16, 128),
      mass.reshape(16, 128), kind.reshape(16, 128))
    return rate.reshape(2, 2, 4, 128), acc.reshape(3, 2, 2, 4, 128)


def solution(mesh):
    in_specs = (
        P(None, "gx", "gy", None, None),
        P(None, "gx", "gy", None, None),
        P("gx", "gy", None, None),
        P("gx", "gy", None, None),
        P("gx", "gy", None, None),
    )
    out_specs = (P("gx", "gy", None, None), P(None, "gx", "gy", None, None))
    return jax.shard_map(functools.partial(local, True), mesh=mesh, in_specs=in_specs, out_specs=out_specs,
                         check_vma=False)
```

time: 71.8 us -> 43.1 us (0.60)
  Pallas kernels: 68.2 us -> 39.6 us
    pallas_call x1, Pallas kernels: 68.2 us -> 39.6 us  [local(): pl.pallas_call(functools.partial(kernel, comm), out_shape=(jax.ShapeDtype...]
where the time goes in v1:
time: 43.1 us; the launch traced here: 42.9 us
  Pallas kernels  39.6 us (92%)
  local copies, waits for them, and re-layouts  2.64 us (6%)
  between operations  0.64 us (1%)
    pallas_call x1, Pallas kernels, local(): pl.pallas_call(functools.partial(kernel, comm), out_shape=(jax.ShapeDtype...  39.6 us
    unnamed x2, local copies, waits for them, and re-layouts  2.64 us

profile of v1, /device:TPU:1, one launch (start us, length us, event | category | flops | bytes accessed | tf_op | source)
XLA Modules:
  0.0 42.9 jit_solution(7566850220017843583)
XLA Ops:
  0.6 39.6 %shard_map.68 = (f32[16,128]{1,0:T(8,128)}, f32[3,16,128]{2,1,0:T(8,128)}) custom-call(f32[3,16,128]{2,1,0:T(8,128)} %bitcast.9, f32[3,16,128]{2,1,0:T(8,128)} %bitcast.10, f32[16,128]{1,0:T(8,128)} %bitcast.11, f32[16,128]{1,0:T(8,128)} %bitcast.12, s32[16,128]{1,0:T(8,128)} %bitcast.13), custom_call_target="tpu_custom_call" | custom-call | flops 2000000000 | bytes 1000000 | tf_op jit(solution)/shard_map/pallas_call | solution.py:385
  40.2 1.3 %copy.9 = f32[2,2,4,128]{3,2,1,0:T(4,128)} copy(f32[2,2,4,128]{3,2,1,0:T(4,128)} %bitcast.8) | data formatting | bytes 16384
  41.5 1.3 %copy.10 = f32[3,2,2,4,128]{4,3,2,1,0:T(4,128)} copy(f32[3,2,2,4,128]{4,3,2,1,0:T(4,128)} %bitcast.7) | data formatting | bytes 49152

commit v2 on v1

--- a/solution.py
+++ b/solution.py
@@ -26,7 +26,9 @@
 BOTH = {0: (0, 1), 1: (2, 3)}
 ONE = {0: 2, 1: 1}
 LANE = {0: 128, 1: 0}
-CUT = 1
+CUT = 2
+WIDTH = 256
+ROWS = 128
 
 
 def pieces(x):
@@ -170,25 +172,27 @@
     def two(x):
         hi = x.astype(BF16)
         lo = (x - hi.astype(F32)).astype(BF16)
-        return jnp.concatenate([hi, lo], axis=0)
+        return hi, lo
 
     def weigh(tc, p, col, full_c, half_c, full_d, half_d, self_col):
-        gap = jnp.dot(far[col], near[tc * 2 + p], preferred_element_type=F32)
-        for k in range(3):
-            d2 = jnp.maximum(gap[:, 256 * k:min(256 * k + 256, 640)], TINY)
+        lhs = far[col]
+        for at in range(0, 640, WIDTH):
+          for r in range(0, 128, ROWS):
+            gap = jnp.dot(lhs[r:r + ROWS], near[tc * 2 + p, :, at:min(at + WIDTH, 640)], preferred_element_type=F32)
+            d2 = jnp.maximum(gap, TINY)
             wedge = jnp.maximum(1.0 - d2 * lax.rsqrt(d2), 0.0)
             c = wedge * wedge * wedge
             d = c * pl.reciprocal(d2 + SOFT4, approx=True)
-            if self_col and k < 2:
-                halves = [d[:, 0:128], d[:, 128:256]]
-                halves[k] = halves[k] * off[...]
-                d = jnp.concatenate(halves, axis=1)
-            if k < 2:
-                full_c[k * 256:k * 256 + 256] = two(c)
-                full_d[k * 256:k * 256 + 256] = two(d)
-            else:
-                half_c[...] = two(c)
-                half_d[...] = two(d)
+            k = at // 256
+            if self_col and k < 2 and at <= 384 * k < at + WIDTH:
+                parts_d = [d[:, j:j + 128] for j in range(0, d.shape[1], 128)]
+                parts_d[(384 * k - at) // 128] *= off[r:r + ROWS]
+                d = jnp.concatenate(parts_d, axis=1)
+            lane = at % 256
+            for (hi, lo), full, half in ((two(c), full_c, half_c), (two(d), full_d, half_d)):
+                out = full.at[k * 256:k * 256 + 256, lane:lane + gap.shape[1]] if k < 2 else half
+                out[r:r + ROWS] = hi
+                out[128 + r:128 + r + ROWS] = lo
 
     def total(feat, rows, p, cols, full, half):
         lf, lh = [], []
@@ -202,10 +206,10 @@
         return (f[:, 0:128], f[:, 128:256] + h) if p == 0 else (f[:, 0:128] + h, f[:, 128:256])
 
     def mates(tc):
-        return [lax.rem(tc + k, 4) for k in range(4)]
+        return [(tc + k) % 4 for k in range(4)]
 
     def halo(tc):
-        a, b = tc // 2, lax.rem(tc, 2)
+        a, b = tc // 2, tc % 2
         return [4 + 2 * a, 5 + 2 * a, 8 + 2 * b, 9 + 2 * b, 12 + tc]
 
     def fold(s):
@@ -215,23 +219,30 @@
     for c in range(4):
         column(c)
 
-    def own_pairs(tc):
+    def own_weights(tc):
         for p in range(2):
             cols = mates(tc)
             for k in range(4):
                 weigh(tc, p, cols[k], cfull.at[p, tc, k], chalf.at[p, tc, k], dfull.at[p, tc, k], dhalf.at[p, tc, k], k == 0)
+
+    def own_sums(tc):
+        for p in range(2):
             for which, (feat, full, half) in enumerate(((feat_c, cfull, chalf), (feat_d, dfull, dhalf))):
-                got = total(feat, 80, p, cols, full[p, tc, 0:4], half[p, tc, 0:4])
+                got = total(feat, 80, p, mates(tc), full[p, tc, 0:4], half[p, tc, 0:4])
                 for h in range(2):
                     sums[tc * 2 + p, h, which * 80:which * 80 + 80] = got[h]
 
-    pl.loop(0, CUT)(own_pairs)
+    for tc in range(CUT):
+        own_weights(tc)
     if comm:
         pl.semaphore_wait(barrier, 8)
         moves = swap(ext, 32, send_sem, recv_sem)
         for c in moves:
             c.start()
-    pl.loop(CUT, 4)(own_pairs)
+    for tc in range(CUT, 4):
+        own_weights(tc)
+    for tc in range(4):
+        own_sums(tc)
     if comm:
         for c in moves:
             c.wait()
@@ -245,22 +256,20 @@
     outside = (below_a & (gx == 0)) | (above_a & (gx == nx - 1)) | (below_b & (gy == 0)) | (above_b & (gy == ny - 1))
     features(16, 48, jnp.logical_not(outside))
 
-    @pl.loop(0, 3)
-    def _(n):
-        for k in range(4):
-            column(4 + n * 4 + k)
-
-    @pl.loop(0, 4)
-    def _(tc):
+    for c in range(4, 16):
+        column(c)
+    for tc in range(4):
         for p in range(2):
             cols = halo(tc)
             for k in range(5):
                 weigh(tc, p, cols[k], cfull.at[p, tc, 4 + k], chalf.at[p, tc, 4 + k], dfull.at[p, tc, k],
                       dhalf.at[p, tc, k], False)
-            got = total(feat_c, 80, p, cols, cfull[p, tc, 4:9], chalf[p, tc, 4:9])
+    for tc in range(4):
+        for p in range(2):
+            got = total(feat_c, 80, p, halo(tc), cfull[p, tc, 4:9], chalf[p, tc, 4:9])
             for h in range(2):
-                base = pl.multiple_of((tc * 4 + p * 2 + h) * 56, 8)
-                parts[pl.ds(base, 24), :] = fold(sums[tc * 2 + p, h, 0:80] + got[h])
+                base = (tc * 4 + p * 2 + h) * 56
+                parts[base:base + 24, :] = fold(sums[tc * 2 + p, h, 0:80] + got[h])
 
     def part(f, stride=56):
         return take_rows(parts, f, stride, 16)
@@ -303,13 +312,12 @@
         for c in moves:
             c.start()
 
-    @pl.loop(0, 4)
-    def _(tc):
+    for tc in range(4):
         for p in range(2):
             got = total(feat_d, 80, p, halo(tc), dfull[p, tc, 0:5], dhalf[p, tc, 0:5])
             for h in range(2):
                 s = sums[tc * 2 + p, h, 80:160] + got[h]
-                base = pl.multiple_of((tc * 4 + p * 2 + h) * 56, 8)
+                base = (tc * 4 + p * 2 + h) * 56
                 parts[pl.ds(base + 24, 24), :] = fold(s)
                 parts[pl.ds(base + 48, 8), :] = s[72:80]
 
@@ -330,8 +338,7 @@
 
     slopes(0, 16, None)
 
-    @pl.loop(0, 4)
-    def _(tc):
+    for tc in range(4):
         for p in range(2):
             got = total(feat_g, 16, p, mates(tc), cfull[p, tc, 0:4], chalf[p, tc, 0:4])
             for h in range(2):
@@ -364,12 +371,11 @@
             c.wait()
     slopes(16, 48, jnp.logical_not(outside))
 
-    @pl.loop(0, 4)
-    def _(tc):
+    for tc in range(4):
         for p in range(2):
             got = total(feat_g, 16, p, halo(tc), cfull[p, tc, 4:9], chalf[p, tc, 4:9])
             for h in range(2):
-                base = pl.multiple_of((tc * 4 + p * 2 + h) * 16, 8)
+                base = (tc * 4 + p * 2 + h) * 16
                 parts[pl.ds(base, 16), :] = gsums[tc * 2 + p, h] + got[h]
 
     q = [part(f, 16) for f in range(12)]
@@ -377,6 +383,21 @@
     spread = spread - (dot3(q, xt) - q[3])
     rate = -rho * flow + DELTA_SOUND * spread
     rate_ref[...] = jnp.where(kind > 0, rate, 0.0)
+
+
+def last(a_ref, b_ref, rate_ref, acc_ref):
+    rate_ref[...] = a_ref[...]
+    acc_ref[...] = b_ref[...]
+
+
+def finish(rate, acc):
+    vmem = pl.BlockSpec(memory_space=pltpu.VMEM)
+    return pl.pallas_call(
+        last,
+        out_shape=(jax.ShapeDtypeStruct((16, 128), F32), jax.ShapeDtypeStruct((3, 16, 128), F32)),
+        in_specs=[vmem, vmem],
+        out_specs=(vmem, vmem),
+    )(rate, acc)
 
 
 def local(comm, positions, velocity, density, mass, kind):
@@ -413,6 +434,7 @@
         cost_estimate=pl.CostEstimate(flops=2 * 10**9, bytes_accessed=10**6, transcendentals=10**7),
     )(positions.reshape(3, 16, 128), velocity.reshape(3, 16, 128), density.reshape(16, 128),
       mass.reshape(16, 128), kind.reshape(16, 128))
+    rate, acc = finish(rate, acc)
     return rate.reshape(2, 2, 4, 128), acc.reshape(3, 2, 2, 4, 128)
 
 

time: 43.1 us -> 38.1 us (0.88)
  local copies, waits for them, and re-layouts: 2.64 us -> 0 us
  Pallas kernels: 39.6 us -> 37.3 us
    pallas_call x1, Pallas kernels: 39.6 us -> 35.9 us  [local(): pl.pallas_call(functools.partial(kernel, comm), out_shape=(jax.ShapeDtype...]
    unnamed x2 -> x0, local copies, waits for them, and re-layouts: 2.64 us -> none
    pallas_call x0 -> x1, Pallas kernels: none -> 1.37 us  [finish(): pl.pallas_call(last, out_shape=(jax.ShapeDtypeStruct((16, 128), F32), jax...]
where the time goes in v2:
time: 38.1 us; the launch traced here: 37.9 us
  Pallas kernels  37.3 us (98%)
  between operations  0.64 us (2%)
    pallas_call x1, Pallas kernels, local(): pl.pallas_call(functools.partial(kernel, comm), out_shape=(jax.ShapeDtype...  35.9 us
    pallas_call x1, Pallas kernels, finish(): pl.pallas_call(last, out_shape=(jax.ShapeDtypeStruct((16, 128), F32), jax...  1.37 us

profile of v2, /device:TPU:1, one launch (start us, length us, event | category | flops | bytes accessed | tf_op | source)
XLA Modules:
  0.0 37.9 jit_solution(4173787843057827873)
XLA Ops:
  0.6 35.9 %shard_map.68 = (f32[16,128]{1,0:T(8,128)}, f32[3,16,128]{2,1,0:T(8,128)}) custom-call(f32[3,16,128]{2,1,0:T(8,128)} %bitcast.7, f32[3,16,128]{2,1,0:T(8,128)} %bitcast.8, f32[16,128]{1,0:T(8,128)} %bitcast.10, f32[16,128]{1,0:T(8,128)} %bitcast.11, s32[16,128]{1,0:T(8,128)} %bitcast.12), custom_call_target="tpu_custom_call" | custom-call | flops 2000000000 | bytes 1000000 | tf_op jit(solution)/shard_map/pallas_call | solution.py:406
  36.6 1.4 %shard_map.69 = (f32[16,128]{1,0:T(8,128)}, f32[3,16,128]{2,1,0:T(8,128)}) custom-call(f32[16,128]{1,0:T(8,128)} %get-tuple-element.6.a_ref, f32[3,16,128]{2,1,0:T(8,128)} %get-tuple-element.7.b_ref), custom_call_target="tpu_custom_call" | custom-call | tf_op jit(solution)/shard_map/pallas_call | solution.py:395

commit v3 on v2

--- a/solution.py
+++ b/solution.py
@@ -20,7 +20,8 @@
 
 F32 = jnp.float32
 BF16 = jnp.bfloat16
-RAW = 80
+RAW = 48
+RAW_D = 32
 SIDES = [(i, j) for i in (-1, 0, 1) for j in (-1, 0, 1) if (i, j) != (0, 0)]
 TINY = 1e-12
 BOTH = {0: (0, 1), 1: (2, 3)}
@@ -94,6 +95,7 @@
 
     def swap(buf, rows, ssem, rsem):
         moves = []
+        kinds = ([], [], [])
         for i, j in SIDES:
             if j == 0:
                 a = 1 if i > 0 else 0
@@ -111,7 +113,8 @@
                     dst_ref=buf.at[pl.ds(dst * rows, count * rows)],
                     send_sem=ssem.at[n], recv_sem=rsem.at[n],
                     device_id=peer(i, j), device_id_type=MESH))
-        return moves
+                kinds[0 if j == 0 else 1 if i == 0 else 2].append(moves[-1])
+        return kinds
 
     ox = ((gx * 2 + 1) * 2).astype(F32)
     oy = ((gy * 2 + 1) * 2).astype(F32)
@@ -131,43 +134,51 @@
     eye16 = jnp.where(eye, 1.0, 0.0).astype(BF16)
     off[...] = jnp.where(eye, 0.0, 1.0)
 
-    def features(first, count, inside):
+    def source(first, count, inside):
         def chan(ch):
             return take_rows(ext, first * 8 + ch, 8, count)
 
         x = [chan(0) - ox, chan(1) - oy, chan(2) - 4.0]
         v = [chan(3 + d) for d in range(3)]
-        r = chan(6)
         w = chan(7)
         if inside is not None:
             w = jnp.where(inside, w, 0.0)
-        pr = power7(r + 1.0)
-        vx = v[0] * x[0] + v[1] * x[1] + v[2] * x[2]
-        wx = [w * x[d] for d in range(3)]
-        wxx = [wx[a] * x[b] for a in range(3) for b in range(a, 3)]
-        wv = [w * v[d] for d in range(3)]
+        return x, v, chan(6), w, [w * x[d] for d in range(3)], [w * v[d] for d in range(3)]
+
+    def features(first, count, inside):
+        x, v, r, w, wx, wv = source(first, count, inside)
         wr = w * r
-        wp = w * pr
+        wp = w * power7(r + 1.0)
         zero = jnp.zeros_like(w)
-        rows = [w] + wx + wxx + [wr] + [wr * x[d] for d in range(3)] + wv + [w * vx] + [wp] + [wp * x[d] for d in range(3)]
-        rows += [zero, zero]
-        e, f = pieces(w), pieces(wr)
-        rows += wv + wx + wxx + [wv[a] * x[b] for a in range(3) for b in range(3)] + [w * vx * x[d] for d in range(3)]
+        rows = [w] + wx + [wx[a] * x[b] for a in range(3) for b in range(a, 3)] + [wr] + [wr * x[d] for d in range(3)]
+        rows += wv + [wv[0] * x[0] + wv[1] * x[1] + wv[2] * x[2]] + [wp] + [wp * x[d] for d in range(3)] + [zero, zero]
+        for f, value in enumerate(rows + distance_rows(x, True)):
+            spread_rows(raw, first * RAW + f, RAW, value)
+
+    def features_d(first, count, inside):
+        x, v, r, w, wx, wv = source(first, count, inside)
+        zero = jnp.zeros_like(w)
+        wvx = wv[0] * x[0] + wv[1] * x[1] + wv[2] * x[2]
+        e, f = pieces(w), pieces(w * r)
+        rows = wv + wx + [wx[a] * x[b] for a in range(3) for b in range(a, 3)]
+        rows += [wv[a] * x[b] for a in range(3) for b in range(3)] + [wvx * x[d] for d in range(3)]
         rows += [e[0], f[0], e[1], f[1], e[2], f[2], zero, zero]
-        rows += distance_rows(x, True)
         for f, value in enumerate(rows):
-            spread_rows(raw, first * RAW + f, RAW, value)
+            spread_rows(raw, first * RAW_D + f, RAW_D, value)
 
     def column(c):
         dist = []
-        for layer in range(4):
-            cell = c * 4 + layer
-            got = raw[pl.ds(pl.multiple_of(cell * RAW, 8), RAW), :]
+        for cell in range(c * 4, c * 4 + 4):
+            got = raw[cell * RAW:cell * RAW + RAW, :]
             feat_c[cell] = jnp.concatenate(list(pieces(got[0:24])) + [jnp.zeros((8, 128), F32)], axis=0).astype(BF16)
-            feat_d[cell] = jnp.concatenate(list(pieces(got[24:48])) + [got[48:56]], axis=0).astype(BF16)
-            dist += [got[56:80], jnp.zeros((8, 128), F32)]
+            dist += [got[24:48], jnp.zeros((8, 128), F32)]
         dist = jnp.concatenate(dist, axis=0).astype(BF16)
         far[c] = lax.dot_general(eye16, dist, (((1,), (1,)), ((), ())), preferred_element_type=F32).astype(BF16)
+
+    def column_d(c):
+        for cell in range(c * 4, c * 4 + 4):
+            got = raw[cell * RAW_D:cell * RAW_D + RAW_D, :]
+            feat_d[cell] = jnp.concatenate(list(pieces(got[0:24])) + [got[24:32]], axis=0).astype(BF16)
 
     def two(x):
         hi = x.astype(BF16)
@@ -227,49 +238,59 @@
 
     def own_sums(tc):
         for p in range(2):
-            for which, (feat, full, half) in enumerate(((feat_c, cfull, chalf), (feat_d, dfull, dhalf))):
-                got = total(feat, 80, p, mates(tc), full[p, tc, 0:4], half[p, tc, 0:4])
-                for h in range(2):
-                    sums[tc * 2 + p, h, which * 80:which * 80 + 80] = got[h]
+            got = total(feat_c, 80, p, mates(tc), cfull[p, tc, 0:4], chalf[p, tc, 0:4])
+            for h in range(2):
+                sums[tc * 2 + p, h] = got[h]
 
     for tc in range(CUT):
         own_weights(tc)
     if comm:
         pl.semaphore_wait(barrier, 8)
         moves = swap(ext, 32, send_sem, recv_sem)
-        for c in moves:
+        for c in moves[2] + moves[1] + moves[0]:
             c.start()
     for tc in range(CUT, 4):
         own_weights(tc)
     for tc in range(4):
         own_sums(tc)
-    if comm:
-        for c in moves:
-            c.wait()
-
     cell = lax.broadcasted_iota(jnp.int32, (48, 128), 0) // 4 + 4
-    group = cell // 2
-    below_a = (group == 2) | (cell == 12) | (cell == 13)
-    above_a = (group == 3) | (cell == 14) | (cell == 15)
-    below_b = (group == 4) | (cell == 12) | (cell == 14)
-    above_b = (group == 5) | (cell == 13) | (cell == 15)
+    pair_of = cell // 2
+    below_a = (pair_of == 2) | (cell == 12) | (cell == 13)
+    above_a = (pair_of == 3) | (cell == 14) | (cell == 15)
+    below_b = (pair_of == 4) | (cell == 12) | (cell == 14)
+    above_b = (pair_of == 5) | (cell == 13) | (cell == 15)
     outside = (below_a & (gx == 0)) | (above_a & (gx == nx - 1)) | (below_b & (gy == 0)) | (above_b & (gy == ny - 1))
-    features(16, 48, jnp.logical_not(outside))
-
-    for c in range(4, 16):
-        column(c)
+    inside = jnp.logical_not(outside)
+
+    def halo_pairs(group, slots):
+        if comm:
+            for c in moves[group]:
+                c.wait()
+        first = 4 + 4 * group
+        features(first * 4, 16, inside[16 * group:16 * group + 16])
+        for c in range(first, first + 4):
+            column(c)
+        for tc in range(4):
+            for p in range(2):
+                cols = halo(tc)
+                for k in slots:
+                    weigh(tc, p, cols[k], cfull.at[p, tc, 4 + k], chalf.at[p, tc, 4 + k], dfull.at[p, tc, 4 + k],
+                          dhalf.at[p, tc, 4 + k], False)
+
+    halo_pairs(0, (0, 1))
     for tc in range(4):
         for p in range(2):
-            cols = halo(tc)
-            for k in range(5):
-                weigh(tc, p, cols[k], cfull.at[p, tc, 4 + k], chalf.at[p, tc, 4 + k], dfull.at[p, tc, k],
-                      dhalf.at[p, tc, k], False)
+            got = total(feat_c, 80, p, halo(tc)[0:2], cfull[p, tc, 4:6], chalf[p, tc, 4:6])
+            for h in range(2):
+                sums[tc * 2 + p, h] += got[h]
+    halo_pairs(1, (2, 3))
+    halo_pairs(2, (4,))
     for tc in range(4):
         for p in range(2):
-            got = total(feat_c, 80, p, halo(tc), cfull[p, tc, 4:9], chalf[p, tc, 4:9])
+            got = total(feat_c, 80, p, halo(tc)[2:5], cfull[p, tc, 6:9], chalf[p, tc, 6:9])
             for h in range(2):
                 base = (tc * 4 + p * 2 + h) * 56
-                parts[base:base + 24, :] = fold(sums[tc * 2 + p, h, 0:80] + got[h])
+                parts[base:base + 24, :] = fold(sums[tc * 2 + p, h] + got[h])
 
     def part(f, stride=56):
         return take_rows(parts, f, stride, 16)
@@ -309,14 +330,20 @@
         spread_rows(gext, d, 4, grad[d])
     if comm:
         moves = swap(gext, 16, gsend_sem, grecv_sem)
-        for c in moves:
+        for c in moves[2] + moves[1] + moves[0]:
             c.start()
 
+    features_d(0, 16, None)
+    features_d(16, 48, inside)
+    for c in range(16):
+        column_d(c)
+
     for tc in range(4):
         for p in range(2):
-            got = total(feat_d, 80, p, halo(tc), dfull[p, tc, 0:5], dhalf[p, tc, 0:5])
+            mine = total(feat_d, 80, p, mates(tc), dfull[p, tc, 0:4], dhalf[p, tc, 0:4])
+            got = total(feat_d, 80, p, halo(tc), dfull[p, tc, 4:9], dhalf[p, tc, 4:9])
             for h in range(2):
-                s = sums[tc * 2 + p, h, 80:160] + got[h]
+                s = mine[h] + got[h]
                 base = (tc * 4 + p * 2 + h) * 56
                 parts[pl.ds(base + 24, 24), :] = fold(s)
                 parts[pl.ds(base + 48, 8), :] = s[72:80]
@@ -366,17 +393,20 @@
         acc_ref[b] = jnp.where(moving, force, 0.0)
     spread = spread - dot3(grad, back)
 
-    if comm:
-        for c in moves:
-            c.wait()
-    slopes(16, 48, jnp.logical_not(outside))
-
-    for tc in range(4):
-        for p in range(2):
-            got = total(feat_g, 16, p, halo(tc), cfull[p, tc, 4:9], chalf[p, tc, 4:9])
-            for h in range(2):
-                base = (tc * 4 + p * 2 + h) * 16
-                parts[pl.ds(base, 16), :] = gsums[tc * 2 + p, h] + got[h]
+    for group, (lo, hi) in enumerate(((0, 2), (2, 4), (4, 5))):
+        if comm:
+            for c in moves[group]:
+                c.wait()
+        slopes(16 + 16 * group, 16, inside[16 * group:16 * group + 16])
+        for tc in range(4):
+            for p in range(2):
+                got = total(feat_g, 16, p, halo(tc)[lo:hi], cfull[p, tc, 4 + lo:4 + hi], chalf[p, tc, 4 + lo:4 + hi])
+                for h in range(2):
+                    if group < 2:
+                        gsums[tc * 2 + p, h] += got[h]
+                    else:
+                        base = (tc * 4 + p * 2 + h) * 16
+                        parts[base:base + 16, :] = gsums[tc * 2 + p, h] + got[h]
 
     q = [part(f, 16) for f in range(12)]
     q = [q[f] + q[f + 4] + q[f + 8] for f in range(4)]
@@ -420,16 +450,16 @@
             pltpu.VMEM((8, 128, 640), BF16),
             pltpu.VMEM((2, 4, 9, 512, 256), BF16),
             pltpu.VMEM((2, 4, 9, 256, 128), BF16),
-            pltpu.VMEM((2, 4, 5, 512, 256), BF16),
-            pltpu.VMEM((2, 4, 5, 256, 128), BF16),
-            pltpu.VMEM((8, 2, 160, 128), F32),
+            pltpu.VMEM((2, 4, 9, 512, 256), BF16),
+            pltpu.VMEM((2, 4, 9, 256, 128), BF16),
+            pltpu.VMEM((8, 2, 80, 128), F32),
             pltpu.VMEM((16 * 56, 128), F32),
             pltpu.VMEM((8, 2, 16, 128), F32),
             pltpu.VMEM((128, 128), F32),
             dma((10,)), dma((10,)), dma((10,)), dma((10,)),
         ],
         compiler_params=pltpu.CompilerParams(
-            vmem_limit_bytes=56 * 1024 * 1024,
+            vmem_limit_bytes=63 * 1024 * 1024,
             **(dict(collective_id=0, has_side_effects=True) if comm else {})),
         cost_estimate=pl.CostEstimate(flops=2 * 10**9, bytes_accessed=10**6, transcendentals=10**7),
     )(positions.reshape(3, 16, 128), velocity.reshape(3, 16, 128), density.reshape(16, 128),

time: 38.1 us -> 36.8 us (0.966)
  Pallas kernels: 37.3 us -> 36 us
    pallas_call x1, Pallas kernels: 35.9 us -> 34.6 us  [local(): pl.pallas_call(functools.partial(kernel, comm), out_shape=(jax.ShapeDtype...]
where the time goes in v3:
time: 36.8 us; the launch traced here: 36.6 us
  Pallas kernels  36 us (98%)
  between operations  0.64 us (2%)
    pallas_call x1, Pallas kernels, local(): pl.pallas_call(functools.partial(kernel, comm), out_shape=(jax.ShapeDtype...  34.6 us
    pallas_call x1, Pallas kernels, finish(): pl.pallas_call(last, out_shape=(jax.ShapeDtypeStruct((16, 128), F32), jax...  1.37 us

profile of v3, /device:TPU:1, one launch (start us, length us, event | category | flops | bytes accessed | tf_op | source)
XLA Modules:
  0.0 36.6 jit_solution(17707353810319020744)
XLA Ops:
  0.6 34.6 %shard_map.68 = (f32[16,128]{1,0:T(8,128)}, f32[3,16,128]{2,1,0:T(8,128)}) custom-call(f32[3,16,128]{2,1,0:T(8,128)} %bitcast.7, f32[3,16,128]{2,1,0:T(8,128)} %bitcast.8, f32[16,128]{1,0:T(8,128)} %bitcast.10, f32[16,128]{1,0:T(8,128)} %bitcast.11, s32[16,128]{1,0:T(8,128)} %bitcast.12), custom_call_target="tpu_custom_call" | custom-call | flops 2000000000 | bytes 1000000 | tf_op jit(solution)/shard_map/pallas_call | solution.py:436
  35.3 1.4 %shard_map.69 = (f32[16,128]{1,0:T(8,128)}, f32[3,16,128]{2,1,0:T(8,128)}) custom-call(f32[16,128]{1,0:T(8,128)} %get-tuple-element.6.a_ref, f32[3,16,128]{2,1,0:T(8,128)} %get-tuple-element.7.b_ref), custom_call_target="tpu_custom_call" | custom-call | tf_op jit(solution)/shard_map/pallas_call | solution.py:425

commit v4 on v3

--- a/solution.py
+++ b/solution.py
@@ -278,16 +278,11 @@
                           dhalf.at[p, tc, 4 + k], False)
 
     halo_pairs(0, (0, 1))
-    for tc in range(4):
-        for p in range(2):
-            got = total(feat_c, 80, p, halo(tc)[0:2], cfull[p, tc, 4:6], chalf[p, tc, 4:6])
-            for h in range(2):
-                sums[tc * 2 + p, h] += got[h]
     halo_pairs(1, (2, 3))
     halo_pairs(2, (4,))
     for tc in range(4):
         for p in range(2):
-            got = total(feat_c, 80, p, halo(tc)[2:5], cfull[p, tc, 6:9], chalf[p, tc, 6:9])
+            got = total(feat_c, 80, p, halo(tc), cfull[p, tc, 4:9], chalf[p, tc, 4:9])
             for h in range(2):
                 base = (tc * 4 + p * 2 + h) * 56
                 parts[base:base + 24, :] = fold(sums[tc * 2 + p, h] + got[h])

time: 36.8 us -> 36.9 us (level)
  no operation moved by 1% of the time
where the time goes in v4:
time: 36.9 us; the launch traced here: 36.7 us
  Pallas kernels  36 us (98%)
  between operations  0.64 us (2%)
    pallas_call x1, Pallas kernels, local(): pl.pallas_call(functools.partial(kernel, comm), out_shape=(jax.ShapeDtype...  34.7 us
    pallas_call x1, Pallas kernels, finish(): pl.pallas_call(last, out_shape=(jax.ShapeDtypeStruct((16, 128), F32), jax...  1.37 us

profile of v4, /device:TPU:1, one launch (start us, length us, event | category | flops | bytes accessed | tf_op | source)
XLA Modules:
  0.0 36.7 jit_solution(17945436192719178657)
XLA Ops:
  0.6 34.7 %shard_map.68 = (f32[16,128]{1,0:T(8,128)}, f32[3,16,128]{2,1,0:T(8,128)}) custom-call(f32[3,16,128]{2,1,0:T(8,128)} %bitcast.7, f32[3,16,128]{2,1,0:T(8,128)} %bitcast.8, f32[16,128]{1,0:T(8,128)} %bitcast.10, f32[16,128]{1,0:T(8,128)} %bitcast.11, s32[16,128]{1,0:T(8,128)} %bitcast.12), custom_call_target="tpu_custom_call" | custom-call | flops 2000000000 | bytes 1000000 | tf_op jit(solution)/shard_map/pallas_call | solution.py:431
  35.3 1.4 %shard_map.69 = (f32[16,128]{1,0:T(8,128)}, f32[3,16,128]{2,1,0:T(8,128)}) custom-call(f32[16,128]{1,0:T(8,128)} %get-tuple-element.6.a_ref, f32[3,16,128]{2,1,0:T(8,128)} %get-tuple-element.7.b_ref), custom_call_target="tpu_custom_call" | custom-call | tf_op jit(solution)/shard_map/pallas_call | solution.py:420
